TPU v7x, 256 devices: a whole 4x4x8 slice. The times are simulated.
256 devices in a mesh: bunch: 16 (over x, y), mp: 16 (over z, core).
Axes of the slice: x: 4, y: 4, z: 8, core: 2. Of those that a mesh axis runs over, the one named last changes fastest.
Arguments:
- phase_space: float32 [4, 256, 65536], P(None, 'bunch', 'mp')
- phase_advance: float32 [2, 256], P(None, 'bunch'), may hold values from 0.3 to 2.8
- centroid_history: float32 [2, 64, 256], P(None, None, 'bunch'), may hold values from -6 to 6
- lr_wake: float32 [16640], replicated, may hold values from -0.046875 to 0.046875
- sr_dipole: float32 [256, 256], replicated, may hold values from -24 to 24
- sr_quad: float32 [256, 256], replicated, may hold values from -24 to 24
- slice_ids: int32 [2, 256, 65536], P(None, 'bunch', 'mp'), may hold values from 0 to 255
Outputs:
- tracked: float32 [4, 256, 65536], P(None, 'bunch', 'mp')
- centroids: float32 [2, 2, 256], P(None, None, 'bunch')
All inputs are finite; a program needn't handle non-finite values.
Results may differ from a plain program's by a relative error of at most 0.00019.
Values sent between devices are 32-bit elements; how exact they have to be, the bound alone decides.
A program may use at most 64 MiB of HBM per device.

v0:
```python
import jax
import jax.numpy as jnp
from jax import lax
from jax.sharding import PartitionSpec as P

SLICES = 256
TURNS = 2
DETUNE = 0.02


def sent_to_all(array, axis):
    copies = jnp.broadcast_to(array, (lax.axis_size(axis), *array.shape))
    return lax.all_to_all(copies, axis, split_axis=0, concat_axis=0, tiled=True)


def over_copies(array, axis):
    everything = sent_to_all(array, axis)
    return jnp.sum(everything, axis=0)


def gather_turned(arrays, axis, dims):
    turned = [jnp.moveaxis(a, dim, 0) for a, dim in zip(arrays, dims)]
    widths = [t[0].size for t in turned]
    both = jnp.concatenate([t.reshape(-1, w) for t, w in zip(turned, widths)], axis=1)
    whole = lax.all_gather(both, axis, axis=0, tiled=True)
    tiles = jnp.split(whole, [sum(widths[:k]) for k in range(1, len(widths))], axis=1)
    return tuple(
        (
            jnp.moveaxis(b.reshape(-1, *t.shape[1:]), 0, dim)
            for b, t, dim in zip(tiles, turned, dims)
        )
    )


def body(phase_space, phase_advance, centroid_history, lr_wake, sr_dipole, sr_quad, slice_ids):
    highest = lax.Precision.HIGHEST
    bunch_dev = phase_space.shape[1]
    depth = centroid_history.shape[1]
    macro_total = phase_space.shape[2] * lax.axis_size("mp")
    all_bunches = bunch_dev * lax.axis_size("bunch")
    length = (depth + 1) * all_bunches
    offset_bunch = lax.axis_index("bunch") * bunch_dev
    own_index = jnp.arange(bunch_dev, dtype=jnp.int32)
    levels = jnp.arange(SLICES, dtype=jnp.int32)
    padded = jnp.concatenate([jnp.zeros((all_bunches,), jnp.float32), lr_wake])
    windows = jax.vmap(lambda start_at: lax.dynamic_slice(padded, (start_at,), (length,)))(
        offset_bunch + own_index
    )
    history = centroid_history

    def moments_of(member):
        slice_line, line_x, line_y = member
        onehot = (slice_line[:, None] == levels[None, :]).astype(jnp.float32)
        stacked = jnp.stack([jnp.ones_like(line_x), line_x, line_y])
        return jnp.dot(stacked, onehot, precision=highest, preferred_element_type=jnp.float32)

    def lookup(member):
        slice_line, kick_rows = member
        onehot = (slice_line[:, None] == levels[None, :]).astype(jnp.float32)
        return lax.dot_general(
            kick_rows,
            onehot,
            (((1,), (1,)), ((), ())),
            precision=highest,
            preferred_element_type=jnp.float32,
        )

    coords = phase_space
    centroid_rows = []
    for turn_index in range(TURNS):
        slice_row = slice_ids[turn_index]
        moments = lax.map(moments_of, (slice_row, coords[0], coords[2]))
        moments = over_copies(moments, "mp")
        density = moments[:, 0] / macro_total
        dipole = jnp.stack([moments[:, 1], moments[:, 2]]) / macro_total
        centroid = jnp.sum(dipole, axis=2)
        centroid_rows.append(centroid)
        dip_kick = jnp.einsum("pbj,ij->pbi", dipole, sr_dipole, precision=highest)
        quad_kick = jnp.einsum("bj,ij->bi", density, sr_quad, precision=highest)
        whole_past, current_all = gather_turned((history, centroid), "bunch", (2, 1))
        all_rows = jnp.concatenate([current_all[:, None, :], whole_past], axis=1)[
            :, :, ::-1
        ].reshape(2, length)
        far_kick = jnp.einsum("bk,pk->pb", windows, all_rows, precision=highest)
        kick_table = jnp.stack([dip_kick[0], dip_kick[1], quad_kick], axis=1)
        picked = lax.map(lookup, (slice_row, kick_table))
        coord_x, moment_x, coord_y, moment_y = (coords[0], coords[1], coords[2], coords[3])
        moment_x = moment_x + picked[:, 0] + picked[:, 2] * coord_x + far_kick[0][:, None]
        moment_y = moment_y + picked[:, 1] - picked[:, 2] * coord_y + far_kick[1][:, None]
        action = coord_x * coord_x + moment_x * moment_x + coord_y * coord_y + moment_y * moment_y
        angle_x = phase_advance[0][:, None] + DETUNE * action
        angle_y = phase_advance[1][:, None] + DETUNE * action
        new_x = jnp.cos(angle_x) * coord_x + jnp.sin(angle_x) * moment_x
        new_mx = -jnp.sin(angle_x) * coord_x + jnp.cos(angle_x) * moment_x
        new_y = jnp.cos(angle_y) * coord_y + jnp.sin(angle_y) * moment_y
        new_my = -jnp.sin(angle_y) * coord_y + jnp.cos(angle_y) * moment_y
        coords = jnp.stack([new_x, new_mx, new_y, new_my])
        history = jnp.concatenate([centroid[:, None, :], history[:, :-1]], axis=1)
    return (coords, jnp.stack(centroid_rows, axis=1))


def solution(mesh):
    placed = (
        P(None, "bunch", "mp"),
        P(None, "bunch"),
        P(None, None, "bunch"),
        P(),
        P(),
        P(),
        P(None, "bunch", "mp"),
    )
    return jax.shard_map(
        body,
        mesh=mesh,
        in_specs=placed,
        out_specs=(P(None, "bunch", "mp"), P(None, None, "bunch")),
        check_vma=False,
    )
```

profile of v0, /device:TPU:96, one launch (start us, length us, event | category | flops | bytes accessed | tf_op | source)
XLA Modules:
  0.0 322.9 jit_solution(3574766325816593291)
XLA Ops:
  1.9 25.5 %while.46 = (s32[]{:T(128)}, f32[16,3,256]{2,0,1:T(8,128)S(1)}, f32[16,4096]{1,0:T(8,128)S(1)}, f32[16,4096]{1,0:T(8,128)S(1)}, s32[16,4096]{1,0:T(8,128)S(1)}, ...) while((s32[]{:T(128)}, f32[16,3,256]{2,0,1:T(8,128)S(1)}, f32[16,4096]{1,0:T(8,128)S(1)}, ...), condition=%wide.region_1.2_spmd.clone, body=%wide.region_0.1_spmd.clone.sunk | while | flops 38821888 | bytes 162961 | solution.py:72
  2.0 1.4 fusion.77
  10.0 1.4 fusion.77
  28.5 7.7 %all-to-all-start = ((f32[16,16,3,256]{3,1,2,0:T(8,128)}), f32[16,16,3,256]{3,1,2,0:T(8,128)S(1)}, u32[]{:S(2)}, u32[]{:S(2)}) async-start(f32[16,16,3,256]{3,1,2,0:T(8,128)} %broadcast_in_dim.39), calls=%async_computation | async-start | bytes 1572864 | tf_op jit(solution)/shard_map/all_to_all | solution.py:13
  36.3 36.2 %while.45 = (s32[]{:T(128)}, f32[16896]{0:T(1024)S(1)}, s32[16,1]{0,1:T(1,128)S(1)}, f32[16,16640]{1,0:T(8,128)S(1)}, s32[]{:T(128)}, /*index=5*/s32[]{:T(128)}) while((s32[]{:T(128)}, f32[16896]{0:T(1024)S(1)}, s32[16,1]{0,1:T(1,128)S(1)}, f32[16,16640]{1,0:T(8,128)S(1)}, s32[]{:T(128)}, /*index=5*/s32[]{:T(128)}) %tuple.122), condition=%wide.while_cond, body=%wide.while_body.sunk | while | flops 2 | bytes 399457 | solution.py:46
  72.9 24.0 %all_gather.6 = f32[256,130]{1,0:T(8,128)S(1)} all-gather(f32[16,130]{1,0:T(8,128)S(1)} %pad_maximum_fusion.5), channel_id=1, replica_groups=mesh['bunch'=16,'mp'=16] {'bunch'}, dimensions={0}, use_global_device_ids=true | all-gather | bytes 141440 | tf_op jit(solution)/shard_map/all_gather | solution.py:25
  99.0 57.1 %while.47 = (s32[]{:T(128)}, f32[16,3,4096]{2,0,1:T(8,128)S(1)}, f32[16,3,256]{2,0,1:T(8,128)S(1)}, s32[16,4096]{1,0:T(8,128)}, s32[]{:T(128)}, /*index=5*/s32[]{:T(128)}) while((s32[]{:T(128)}, f32[16,3,4096]{2,0,1:T(8,128)S(1)}, f32[16,3,256]{2,0,1:T(8,128)S(1)}, s32[16,4096]{1,0:T(8,128)}, s32[]{:T(128)}, ...), condition=%wide.region_4.5_spmd.clone, body=%wide.region_3.4_spmd.clone.sunk | while | flops 38797312 | bytes 304217 | solution.py:86
  99.9 2.1 convolution_bitcast_fusion.6
  103.5 2.1 convolution_bitcast_fusion.6
  107.1 2.1 convolution_bitcast_fusion.6
  110.6 2.1 convolution_bitcast_fusion.6
  114.2 2.1 convolution_bitcast_fusion.6
  117.8 2.1 convolution_bitcast_fusion.6
  121.4 2.1 convolution_bitcast_fusion.6
  124.9 2.1 convolution_bitcast_fusion.6
  128.5 2.1 convolution_bitcast_fusion.6
  132.1 2.1 convolution_bitcast_fusion.6
  135.6 2.1 convolution_bitcast_fusion.6
  139.2 2.1 convolution_bitcast_fusion.6
  142.8 2.1 convolution_bitcast_fusion.6
  146.3 2.1 convolution_bitcast_fusion.6
  149.9 2.1 convolution_bitcast_fusion.6
  153.5 2.1 convolution_bitcast_fusion.6
  156.1 2.2 fusion.64
  158.4 3.0 multiply_add_fusion.5
  161.4 40.9 %while.48 = (s32[]{:T(128)}, f32[16,3,256]{2,0,1:T(8,128)S(1)}, f32[16,4096]{1,0:T(8,128)}, f32[16,4096]{1,0:T(8,128)}, s32[16,4096]{1,0:T(8,128)S(1)}, /*index=5*/s32[]{:T(128)}, f32[]{:T(128)}, f32[]{:T(128)}, s32[]{:T(128)}) while((s32[]{:T(128)}, f32[16,3,256]{2,0,1:T(8,128)S(1)}, f32[16,4096]{1,0:T(8,128)}, ...), condition=%wide.region_7.8_spmd.clone, body=%wide.region_6.7_spmd.clone.sunk | while | flops 38821888 | bytes 162961 | solution.py:72
  203.3 7.2 %all-to-all-start.1 = ((f32[16,16,3,256]{3,1,2,0:T(8,128)}), f32[16,16,3,256]{3,1,2,0:T(8,128)}, u32[]{:S(2)}, u32[]{:S(2)}) async-start(f32[16,16,3,256]{3,1,2,0:T(8,128)} %broadcast_in_dim.41), calls=%async_computation.1 | async-start | bytes 1572864 | tf_op jit(solution)/shard_map/all_to_all | solution.py:13
  211.8 19.5 %all-to-all-done.1 = f32[16,16,3,256]{3,1,2,0:T(8,128)} async-done(((f32[16,16,3,256]{3,1,2,0:T(8,128)}), f32[16,16,3,256]{3,1,2,0:T(8,128)}, u32[]{:S(2)}, u32[]{:S(2)}) %all-to-all-start.1) | async-done | bytes 786464 | tf_op jit(solution)/shard_map/all_to_all | solution.py:13
  232.7 23.3 %all_gather.7 = f32[256,130]{1,0:T(8,128)S(1)} all-gather(f32[16,130]{1,0:T(8,128)S(1)} %pad_maximum_fusion.6), channel_id=1, replica_groups=mesh['bunch'=16,'mp'=16] {'bunch'}, dimensions={0}, use_global_device_ids=true | all-gather | bytes 141440 | tf_op jit(solution)/shard_map/all_gather | solution.py:25
  258.7 57.1 %while.49 = (s32[]{:T(128)}, f32[16,3,4096]{2,0,1:T(8,128)S(1)}, f32[16,3,256]{2,0,1:T(8,128)S(1)}, s32[16,4096]{1,0:T(8,128)}, s32[]{:T(128)}, /*index=5*/s32[]{:T(128)}) while((s32[]{:T(128)}, f32[16,3,4096]{2,0,1:T(8,128)S(1)}, f32[16,3,256]{2,0,1:T(8,128)S(1)}, s32[16,4096]{1,0:T(8,128)}, s32[]{:T(128)}, ...), condition=%wide.region_10.11_spmd.clone, body=%wide.region_9.10_spmd.clone.sunk | while | flops 38797312 | bytes 304217 | solution.py:86
  259.7 2.1 convolution_bitcast_fusion.7
  263.2 2.1 convolution_bitcast_fusion.7
  266.8 2.1 convolution_bitcast_fusion.7
  270.4 2.1 convolution_bitcast_fusion.7
  273.9 2.1 convolution_bitcast_fusion.7
  277.5 2.1 convolution_bitcast_fusion.7
  281.1 2.1 convolution_bitcast_fusion.7
  284.7 2.1 convolution_bitcast_fusion.7
  288.2 2.1 convolution_bitcast_fusion.7
  291.8 2.1 convolution_bitcast_fusion.7
  295.4 2.1 convolution_bitcast_fusion.7
  298.9 2.1 convolution_bitcast_fusion.7
  302.5 2.1 convolution_bitcast_fusion.7
  306.1 2.1 convolution_bitcast_fusion.7
  309.6 2.1 convolution_bitcast_fusion.7
  313.2 2.1 convolution_bitcast_fusion.7
  316.4 3.2 %multiply_add_fusion.3 = (f32[1,16,4096]{2,1,0:T(8,128)S(1)}, f32[1,16,4096]{2,1,0:T(8,128)S(1)}, f32[1,16,4096]{2,1,0:T(8,128)S(1)}, f32[1,16,4096]{2,1,0:T(8,128)S(1)}, f32[1,16,4096]{2,1,0:T(8,128)S(1)}) fusion(f32[16]{0:T(128)S(1)} %get-tuple-element.282, f32[16]{0:T(128)S(1)} %get-tuple-element.280, f32[16,3,4096]{2,0,1:T(8,128)S(1)} %get-tuple-element.123, ...), kind=kLoop, calls=%fused_computation.77 | loop fusion | flops 2359296 | bytes 3408128 | tf_op jit(solution)/shard_map/add | solution.py:93
  319.7 2.2 multiply_add_fusion.1
  (463 shorter events, 155.2 us)
Async XLA Ops:
  0.6 97.9 %copy-start = (f32[256,256]{1,0:T(8,128)S(1)}, f32[256,256]{1,0:T(8,128)}, u32[]{:S(2)}) copy-start(f32[256,256]{1,0:T(8,128)} %param.19) | copy-start | bytes 786436
  0.6 1.2 copy-start.8
  27.5 1.0 copy-start.7
  27.5 8.7 %copy-start.10 = (f32[2,64,16]{1,2,0:T(8,128)S(1)}, f32[2,64,16]{1,2,0:T(8,128)}, u32[]{:S(2)}) copy-start(f32[2,64,16]{1,2,0:T(8,128)} %param.17) | copy-start | bytes 24580
  27.5 8.8 %copy-start.9 = (f32[16640]{0:T(1024)S(1)}, f32[16640]{0:T(1024)}, u32[]{:S(2)}) copy-start(f32[16640]{0:T(1024)} %param.18) | copy-start | bytes 199684
  28.5 44.1 %all-to-all-start = ((f32[16,16,3,256]{3,1,2,0:T(8,128)}), f32[16,16,3,256]{3,1,2,0:T(8,128)S(1)}, u32[]{:S(2)}, u32[]{:S(2)}) async-start(f32[16,16,3,256]{3,1,2,0:T(8,128)} %broadcast_in_dim.39), calls=%async_computation | async-start | bytes 1572864 | tf_op jit(solution)/shard_map/all_to_all | solution.py:13
  72.7 25.6 %copy-start.4 = (f32[256,256]{1,0:T(8,128)S(1)}, f32[256,256]{1,0:T(8,128)}, u32[]{:S(2)}) copy-start(f32[256,256]{1,0:T(8,128)} %param.20) | copy-start | bytes 786436
  156.1 2.3 copy-start.11
  156.1 2.3 copy-start.1
  202.3 1.0 copy-start.6
  203.3 28.0 %all-to-all-start.1 = ((f32[16,16,3,256]{3,1,2,0:T(8,128)}), f32[16,16,3,256]{3,1,2,0:T(8,128)}, u32[]{:S(2)}, u32[]{:S(2)}) async-start(f32[16,16,3,256]{3,1,2,0:T(8,128)} %broadcast_in_dim.41), calls=%async_computation.1 | async-start | bytes 1572864 | tf_op jit(solution)/shard_map/all_to_all | solution.py:13
  211.8 44.2 %copy-start.5 = (f32[256,256]{1,0:T(8,128)S(1)}, f32[256,256]{1,0:T(8,128)}, u32[]{:S(2)}) copy-start(f32[256,256]{1,0:T(8,128)} %param.20) | copy-start | bytes 786436
  258.6 57.8 %copy-start.2 = (f32[1,16,4096]{2,1,0:T(8,128)S(1)}, f32[1,16,4096]{2,1,0:T(8,128)}, u32[]{:S(2)}) copy-start(f32[1,16,4096]{2,1,0:T(8,128)} %get-tuple-element.256) | copy-start | bytes 786436
  258.7 57.8 %copy-start.3 = (f32[1,16,4096]{2,1,0:T(8,128)S(1)}, f32[1,16,4096]{2,1,0:T(8,128)}, u32[]{:S(2)}) copy-start(f32[1,16,4096]{2,1,0:T(8,128)} %get-tuple-element.257) | copy-start | bytes 786436
where the time goes:
time: 324 us; the launch traced here: 323 us
  matrix products  119 us (37%)
  local copies, waits for them, and re-layouts  106 us (33%)
  blocking collectives  47.3 us (15%)
  waiting for transfers between devices  19.5 us (6%)
  starting transfers between devices  14.9 us (5%)
  other arithmetic  12.1 us (4%)
  loops' own time  3.33 us (1%)
    dot_general x32, matrix products, lookup(): lax.dot_general(kick_rows, onehot, (((1,), (1,)), ((), ())), precision=hi...  68 us
    all_gather x2, blocking collectives, gather_turned(): whole = lax.all_gather(both, axis, axis=0, tiled=True)  47.3 us
    dynamic_slice x96, local copies, waits for them, and re-layouts, body(): moments = lax.map(moments_of, (slice_row, coords[0], coords[2]))  46.7 us
    dot_general x32, matrix products, moments_of(): jnp.dot(stacked, onehot, precision=highest, preferred_element_type=jnp.fl...  46.3 us
    gather x64, local copies, waits for them, and re-layouts  35.7 us
    all_to_all x2, waiting for transfers between devices, sent_to_all(): return lax.all_to_all(copies, axis, split_axis=0, concat_axis=0, tiled=True)  19.5 us
    all_to_all x2, starting transfers between devices, sent_to_all(): return lax.all_to_all(copies, axis, split_axis=0, concat_axis=0, tiled=True)  14.9 us
    dynamic_update_slice x64, local copies, waits for them, and re-layouts, body(): picked = lax.map(lookup, (slice_row, kick_table))  14.9 us
  transfers between devices with their start and end apart: 2, of which 1 were waited for; matrix products, arithmetic and copies ran while one was open for 11% of the time, Pallas kernels for 0%

commit v1 on v0

--- a/solution.py
+++ b/solution.py
@@ -22,7 +22,9 @@
     turned = [jnp.moveaxis(a, dim, 0) for a, dim in zip(arrays, dims)]
     widths = [t[0].size for t in turned]
     both = jnp.concatenate([t.reshape(-1, w) for t, w in zip(turned, widths)], axis=1)
-    whole = lax.all_gather(both, axis, axis=0, tiled=True)
+    f_now = jnp.stack(lax.axis_size(axis) * [both], 0)
+    right_arr = lax.all_to_all(f_now, axis, 0, 0)
+    whole = jnp.concatenate(right_arr, 0)
     tiles = jnp.split(whole, [sum(widths[:k]) for k in range(1, len(widths))], axis=1)
     return tuple(
         (

time: 324 us -> 313 us (0.966); the launches traced: 323 us -> 307 us
  blocking collectives: 47.3 us -> 0 us
  starting transfers between devices: 14.9 us -> 29.2 us
  local copies, waits for them, and re-layouts: 106 us -> 120 us
    all_gather x2 -> x0, blocking collectives: 47.3 us -> none  [gather_turned(): whole = lax.all_gather(both, axis, axis=0, tiled=True)]
    all_to_all x0 -> x2, starting transfers between devices: none -> 14.3 us  [gather_turned(): right_arr = lax.all_to_all(f_now, axis, 0, 0)]
    rev x2, local copies, waits for them, and re-layouts: 0.67 us -> 5.84 us  [body(): jnp.concatenate([current_all[:, None, :], whole_past], axis=1)[:, :, ::-1]]
  transfers between devices with their start and end apart: 2 -> 4, of which waited for: 1 -> 1; matrix products, arithmetic and copies ran while one was open for 11% -> 49% of each run, Pallas kernels for 0% -> 0%
where the time goes in v1:
time: 313 us; the launch traced here: 307 us
  local copies, waits for them, and re-layouts  120 us (38%)
  matrix products  119 us (38%)
  starting transfers between devices  29.2 us (9%)
  waiting for transfers between devices  19.5 us (6%)
  other arithmetic  15.2 us (5%)
  loops' own time  3.35 us (1%)
    dot_general x32, matrix products, lookup(): lax.dot_general(kick_rows, onehot, (((1,), (1,)), ((), ())), precision=hi...  68 us
    dynamic_slice x96, local copies, waits for them, and re-layouts, body(): moments = lax.map(moments_of, (slice_row, coords[0], coords[2]))  46.6 us
    dot_general x32, matrix products, moments_of(): jnp.dot(stacked, onehot, precision=highest, preferred_element_type=jnp.fl...  46.3 us
    gather x64, local copies, waits for them, and re-layouts  36.1 us
    all_to_all x2, waiting for transfers between devices, sent_to_all(): return lax.all_to_all(copies, axis, split_axis=0, concat_axis=0, tiled=True)  19.5 us
    all_to_all x2, starting transfers between devices, sent_to_all(): return lax.all_to_all(copies, axis, split_axis=0, concat_axis=0, tiled=True)  14.9 us
    dynamic_update_slice x64, local copies, waits for them, and re-layouts, body(): picked = lax.map(lookup, (slice_row, kick_table))  14.9 us
    all_to_all x2, starting transfers between devices, gather_turned(): right_arr = lax.all_to_all(f_now, axis, 0, 0)  14.3 us
  transfers between devices with their start and end apart: 4, of which 1 were waited for; matrix products, arithmetic and copies ran while one was open for 49% of the time, Pallas kernels for 0%

profile of v1, /device:TPU:96, one launch (start us, length us, event | category | flops | bytes accessed | tf_op | source)
XLA Modules:
  0.0 307.0 jit_solution(11033215823786602442)
XLA Ops:
  1.9 25.5 %while.46 = (s32[]{:T(128)}, f32[16,3,256]{2,0,1:T(8,128)S(1)}, f32[16,4096]{1,0:T(8,128)S(1)}, f32[16,4096]{1,0:T(8,128)S(1)}, s32[16,4096]{1,0:T(8,128)S(1)}, ...) while((s32[]{:T(128)}, f32[16,3,256]{2,0,1:T(8,128)S(1)}, f32[16,4096]{1,0:T(8,128)S(1)}, ...), condition=%wide.region_1.2_spmd.clone, body=%wide.region_0.1_spmd.clone.sunk | while | flops 38821888 | bytes 162961 | solution.py:74
  28.5 7.7 %all-to-all-start = ((f32[16,16,3,256]{3,1,2,0:T(8,128)}), f32[16,16,3,256]{3,1,2,0:T(8,128)S(1)}, u32[]{:S(2)}, u32[]{:S(2)}) async-start(f32[16,16,3,256]{3,1,2,0:T(8,128)} %broadcast_in_dim.39), calls=%async_computation | async-start | bytes 1572864 | tf_op jit(solution)/shard_map/all_to_all | solution.py:13
  36.3 36.6 %while.45 = (s32[]{:T(128)}, f32[16896]{0:T(1024)S(1)}, s32[16,1]{0,1:T(1,128)S(1)}, f32[16,16640]{1,0:T(8,128)S(1)}, s32[]{:T(128)}, /*index=5*/s32[]{:T(128)}) while((s32[]{:T(128)}, f32[16896]{0:T(1024)S(1)}, s32[16,1]{0,1:T(1,128)S(1)}, f32[16,16640]{1,0:T(8,128)S(1)}, s32[]{:T(128)}, /*index=5*/s32[]{:T(128)}) %tuple.125), condition=%wide.while_cond, body=%wide.while_body.sunk | while | flops 2 | bytes 399457 | solution.py:48
  74.0 7.0 %all-to-all-start.1 = ((f32[16,16,130]{2,1,0:T(8,128)}), f32[16,16,130]{2,1,0:T(8,128)S(1)}, u32[]{:S(2)}, u32[]{:S(2)}) async-start(f32[16,16,130]{2,1,0:T(8,128)} %stack.35), calls=%async_computation.1 | async-start | bytes 524288 | tf_op jit(solution)/shard_map/all_to_all | solution.py:26
  81.8 57.1 %while.47 = (s32[]{:T(128)}, f32[16,3,4096]{2,0,1:T(8,128)S(1)}, f32[16,3,256]{2,0,1:T(8,128)S(1)}, s32[16,4096]{1,0:T(8,128)}, s32[]{:T(128)}, /*index=5*/s32[]{:T(128)}) while((s32[]{:T(128)}, f32[16,3,4096]{2,0,1:T(8,128)S(1)}, f32[16,3,256]{2,0,1:T(8,128)S(1)}, s32[16,4096]{1,0:T(8,128)}, s32[]{:T(128)}, ...), condition=%wide.region_4.5_spmd.clone, body=%wide.region_3.4_spmd.clone.sunk | while | flops 38797312 | bytes 304217 | solution.py:88
  82.8 2.1 convolution_bitcast_fusion.6
  86.3 2.1 convolution_bitcast_fusion.6
  89.9 2.1 convolution_bitcast_fusion.6
  93.5 2.1 convolution_bitcast_fusion.6
  97.0 2.1 convolution_bitcast_fusion.6
  100.6 2.1 convolution_bitcast_fusion.6
  104.2 2.1 convolution_bitcast_fusion.6
  107.7 2.1 convolution_bitcast_fusion.6
  111.3 2.1 convolution_bitcast_fusion.6
  114.9 2.1 convolution_bitcast_fusion.6
  118.4 2.1 convolution_bitcast_fusion.6
  122.0 2.1 convolution_bitcast_fusion.6
  125.6 2.1 convolution_bitcast_fusion.6
  129.1 2.1 convolution_bitcast_fusion.6
  132.7 2.1 convolution_bitcast_fusion.6
  136.3 2.1 convolution_bitcast_fusion.6
  141.2 2.9 rev.6
  147.1 3.1 multiply_add_fusion.5
  150.2 40.9 %while.48 = (s32[]{:T(128)}, f32[16,3,256]{2,0,1:T(8,128)S(1)}, f32[16,4096]{1,0:T(8,128)}, f32[16,4096]{1,0:T(8,128)}, s32[16,4096]{1,0:T(8,128)S(1)}, /*index=5*/s32[]{:T(128)}, f32[]{:T(128)}, f32[]{:T(128)}, s32[]{:T(128)}) while((s32[]{:T(128)}, f32[16,3,256]{2,0,1:T(8,128)S(1)}, f32[16,4096]{1,0:T(8,128)}, ...), condition=%wide.region_7.8_spmd.clone, body=%wide.region_6.7_spmd.clone.sunk | while | flops 38821888 | bytes 162961 | solution.py:74
  192.1 7.2 %all-to-all-start.2 = ((f32[16,16,3,256]{3,1,2,0:T(8,128)}), f32[16,16,3,256]{3,1,2,0:T(8,128)}, u32[]{:S(2)}, u32[]{:S(2)}) async-start(f32[16,16,3,256]{3,1,2,0:T(8,128)} %broadcast_in_dim.41), calls=%async_computation.2 | async-start | bytes 1572864 | tf_op jit(solution)/shard_map/all_to_all | solution.py:13
  200.6 19.5 %all-to-all-done.2 = f32[16,16,3,256]{3,1,2,0:T(8,128)} async-done(((f32[16,16,3,256]{3,1,2,0:T(8,128)}), f32[16,16,3,256]{3,1,2,0:T(8,128)}, u32[]{:S(2)}, u32[]{:S(2)}) %all-to-all-start.2) | async-done | bytes 786464 | tf_op jit(solution)/shard_map/all_to_all | solution.py:13
  223.8 7.3 %all-to-all-start.3 = ((f32[16,16,130]{2,1,0:T(8,128)}), f32[16,16,130]{2,1,0:T(8,128)}, u32[]{:S(2)}, u32[]{:S(2)}) async-start(f32[16,16,130]{2,1,0:T(8,128)} %stack.39), calls=%async_computation.3 | async-start | bytes 524288 | tf_op jit(solution)/shard_map/all_to_all | solution.py:26
  231.2 57.1 %while.49 = (s32[]{:T(128)}, f32[16,3,4096]{2,0,1:T(8,128)S(1)}, f32[16,3,256]{2,0,1:T(8,128)S(1)}, s32[16,4096]{1,0:T(8,128)}, s32[]{:T(128)}, /*index=5*/s32[]{:T(128)}) while((s32[]{:T(128)}, f32[16,3,4096]{2,0,1:T(8,128)S(1)}, f32[16,3,256]{2,0,1:T(8,128)S(1)}, s32[16,4096]{1,0:T(8,128)}, s32[]{:T(128)}, ...), condition=%wide.region_10.11_spmd.clone, body=%wide.region_9.10_spmd.clone.sunk | while | flops 38797312 | bytes 304217 | solution.py:88
  232.1 2.1 convolution_bitcast_fusion.7
  235.7 2.1 convolution_bitcast_fusion.7
  239.3 2.1 convolution_bitcast_fusion.7
  242.8 2.1 convolution_bitcast_fusion.7
  246.4 2.1 convolution_bitcast_fusion.7
  250.0 2.1 convolution_bitcast_fusion.7
  253.5 2.1 convolution_bitcast_fusion.7
  257.1 2.1 convolution_bitcast_fusion.7
  260.7 2.1 convolution_bitcast_fusion.7
  264.3 2.1 convolution_bitcast_fusion.7
  267.8 2.1 convolution_bitcast_fusion.7
  271.4 2.1 convolution_bitcast_fusion.7
  275.0 2.1 convolution_bitcast_fusion.7
  278.5 2.1 convolution_bitcast_fusion.7
  282.1 2.1 convolution_bitcast_fusion.7
  285.7 2.1 convolution_bitcast_fusion.7
  291.4 1.7 copy.73
  295.3 2.9 rev.7
  300.5 3.3 %multiply_add_fusion.3 = (f32[1,16,4096]{2,1,0:T(8,128)S(1)}, f32[1,16,4096]{2,1,0:T(8,128)S(1)}, f32[1,16,4096]{2,1,0:T(8,128)S(1)}, f32[1,16,4096]{2,1,0:T(8,128)S(1)}, f32[1,16,4096]{2,1,0:T(8,128)S(1)}) fusion(f32[16]{0:T(128)S(1)} %copy-done.16, f32[16]{0:T(128)S(1)} %get-tuple-element.290, f32[16,3,4096]{2,0,1:T(8,128)S(1)} %get-tuple-element.123, ...), kind=kLoop, calls=%fused_computation.77 | loop fusion | flops 2359296 | bytes 3408128 | tf_op jit(solution)/shard_map/add | solution.py:95
  303.8 2.2 multiply_add_fusion.1
  (477 shorter events, 169.9 us)
Async XLA Ops:
  0.6 80.7 %copy-start = (f32[256,256]{1,0:T(8,128)S(1)}, f32[256,256]{1,0:T(8,128)}, u32[]{:S(2)}) copy-start(f32[256,256]{1,0:T(8,128)} %param.19) | copy-start | bytes 786436
  0.6 1.2 copy-start.7
  27.5 1.0 copy-start.6
  27.5 8.7 %copy-start.9 = (f32[2,64,16]{1,2,0:T(8,128)S(1)}, f32[2,64,16]{1,2,0:T(8,128)}, u32[]{:S(2)}) copy-start(f32[2,64,16]{1,2,0:T(8,128)} %param.17) | copy-start | bytes 24580
  27.5 8.8 %copy-start.8 = (f32[16640]{0:T(1024)S(1)}, f32[16640]{0:T(1024)}, u32[]{:S(2)}) copy-start(f32[16640]{0:T(1024)} %param.18) | copy-start | bytes 199684
  28.5 44.5 %all-to-all-start = ((f32[16,16,3,256]{3,1,2,0:T(8,128)}), f32[16,16,3,256]{3,1,2,0:T(8,128)S(1)}, u32[]{:S(2)}, u32[]{:S(2)}) async-start(f32[16,16,3,256]{3,1,2,0:T(8,128)} %broadcast_in_dim.39), calls=%async_computation | async-start | bytes 1572864 | tf_op jit(solution)/shard_map/all_to_all | solution.py:13
  73.0 8.1 %copy-start.4 = (f32[256,256]{1,0:T(8,128)S(1)}, f32[256,256]{1,0:T(8,128)}, u32[]{:S(2)}) copy-start(f32[256,256]{1,0:T(8,128)} %param.20) | copy-start | bytes 786436
  73.1 0.8 copy-start.11
  74.0 64.9 %all-to-all-start.1 = ((f32[16,16,130]{2,1,0:T(8,128)}), f32[16,16,130]{2,1,0:T(8,128)S(1)}, u32[]{:S(2)}, u32[]{:S(2)}) async-start(f32[16,16,130]{2,1,0:T(8,128)} %stack.35), calls=%async_computation.1 | async-start | bytes 524288 | tf_op jit(solution)/shard_map/all_to_all | solution.py:26
  139.7 7.4 %copy-start.1 = (f32[4,16,4096]{2,1,0:T(8,128)S(1)}, f32[4,16,4096]{2,1,0:T(8,128)}, u32[]{:S(2)}) copy-start(f32[4,16,4096]{2,1,0:T(8,128)} %param.15) | copy-start | bytes 3145732
  147.1 3.1 %copy-start.13 = (f32[16]{0:T(128)}, f32[16]{0:T(128)S(1)}, u32[]{:S(2)}) copy-start(f32[16]{0:T(128)S(1)} %get-tuple-element.291) | copy-start | bytes 196
  147.1 3.1 %copy-start.15 = (f32[16]{0:T(128)}, f32[16]{0:T(128)S(1)}, u32[]{:S(2)}) copy-start(f32[16]{0:T(128)S(1)} %get-tuple-element.292) | copy-start | bytes 196
  191.1 1.0 copy-start.5
  191.1 8.2 %copy-start.12 = (f32[2,16]{1,0:T(2,128)S(1)}, f32[2,16]{1,0:T(2,128)}, u32[]{:S(2)}) copy-start(f32[2,16]{1,0:T(2,128)} %copy-done.11) | copy-start | bytes 388
  191.1 8.3 %copy-start.10 = (f32[2,64,16]{1,2,0:T(8,128)S(1)}, f32[2,64,16]{1,2,0:T(8,128)}, u32[]{:S(2)}) copy-start(f32[2,64,16]{1,2,0:T(8,128)} %param.17) | copy-start | bytes 24580
  192.1 28.0 %all-to-all-start.2 = ((f32[16,16,3,256]{3,1,2,0:T(8,128)}), f32[16,16,3,256]{3,1,2,0:T(8,128)}, u32[]{:S(2)}, u32[]{:S(2)}) async-start(f32[16,16,3,256]{3,1,2,0:T(8,128)} %broadcast_in_dim.41), calls=%async_computation.2 | async-start | bytes 1572864 | tf_op jit(solution)/shard_map/all_to_all | solution.py:13
  223.8 65.1 %all-to-all-start.3 = ((f32[16,16,130]{2,1,0:T(8,128)}), f32[16,16,130]{2,1,0:T(8,128)}, u32[]{:S(2)}, u32[]{:S(2)}) async-start(f32[16,16,130]{2,1,0:T(8,128)} %stack.39), calls=%async_computation.3 | async-start | bytes 524288 | tf_op jit(solution)/shard_map/all_to_all | solution.py:26
  293.7 6.8 %copy-start.14 = (f32[16]{0:T(128)S(1)}, f32[16]{0:T(128)}, u32[]{:S(2)}) copy-start(f32[16]{0:T(128)} %copy-done.13) | copy-start | bytes 196
  293.7 6.8 %copy-start.16 = (f32[16]{0:T(128)S(1)}, f32[16]{0:T(128)}, u32[]{:S(2)}) copy-start(f32[16]{0:T(128)} %copy-done.15) | copy-start | bytes 196
  298.2 2.3 copy-start.2
  298.2 2.3 copy-start.3
